TPU v7x, 32 devices: a whole 2x2x4 slice. The times are simulated.
32 devices in a mesh: row: 8 (over z, y), col: 4 (over x, core).
Axes of the slice: x: 2, y: 2, z: 4, core: 2. Of those that a mesh axis runs over, the one named last changes fastest.
Arguments:
- a_send: bfloat16 [2, 32, 32, 128, 128], P(None, ('row', 'col')), may hold values from -6 to 6
- a_where: int32 [2, 32, 32], P(None, ('row', 'col')), may hold values from -1 to 255, as said below
- b_strips: bfloat16 [8, 4, 16, 8, 128, 128], P('row', 'col'), may hold values from -0.25 to 0.25
- b_cols: int32 [8, 4, 16, 8], P('row', 'col'), may hold values from -1 to 7, as said below
Outputs:
- c_panel: bfloat16 [16384, 4096], P('row', 'col')
Inputs may be any that keep to these rules, and one draw needn't show every extreme that they name: `a_where`: positions named within one panel half of one grid device are distinct. Each panel half of each grid device has at least 12 and at most 24 named slots, and in every draw some have exactly 24. `b_cols`: block columns named within one block row of one panel are distinct. Each block row has at least 4 named slots, and in every draw some have exactly 8; the named slots lie anywhere in the row.
All inputs are finite; a program needn't handle non-finite values.
Results may differ from a plain program's by a relative error of at most 0.001.
Values may be sent and summed in bfloat16 or wider, within the bound.
No kernel may reach another device: no remote copies, remote signals or barrier semaphores. Data moves between devices by JAX's collectives and lax.ppermute only.
A program may use at most 128 MiB of HBM per device.

v0:
```python
import functools

import jax
import jax.numpy as jnp
from jax import lax
from jax.experimental import pallas as pl
from jax.experimental.pallas import tpu as pltpu
from jax.sharding import PartitionSpec as P

RB = 16
KB = 16
NJ = 8
PARTS = (66, 26, 8, 8, 20)
ALWAYS = PARTS[0] + PARTS[1]
LENT = 16
GROUP = 4
IN_SMEM = pl.BlockSpec(memory_space=pltpu.SMEM)
ANYWHERE = pl.BlockSpec(memory_space=pl.ANY)
LIMIT = 24 * 1024 * 1024


def in_hbm(value):
    return pltpu.with_memory_space_constraint(value, pltpu.HBM)


def places_in(table, half, owner):
    at = half * table.shape[0] + owner
    return lambda source: table[source, 1 + at // 128, at % 128]


def columns_in(table, rcap, device):
    return lambda slot: table[device, 0, slot % rcap * KB + slot // rcap]


def mark_rows(place, slots, named):
    def reset(j, carry):
        named[j] = 0
        return carry

    def mark(s, carry):
        here = place(s)

        @pl.when(here >= 0)
        def _():
            named[here % KB] = named[here % KB] + 1

        return carry

    lax.fori_loop(0, KB, reset, 0)
    lax.fori_loop(0, slots, mark, 0)


def for_wanted(column, named, rcap, action):
    def visit(slot, number):
        wanted = column(slot) >= 0

        @pl.when(wanted)
        def _():
            action(slot, number)

        return number + wanted.astype(jnp.int32)

    def visit_row(j, match, number):
        return lax.fori_loop(j * rcap, jnp.where(match, (j + 1) * rcap, j * rcap), visit, number)

    count = lax.fori_loop(0, KB, lambda j, n: visit_row(j, named[j] > 1, n), jnp.int32(0))
    return lax.fori_loop(0, KB, lambda j, n: visit_row(j, named[j] == 1, n), count)


def pack_main(spot, tables, strips, guests, *refs):
    early, late, stage, table, sem_table, named, sem, sem_out = refs[-8:]
    shift = spot[5]
    stop = stage.shape[0] - shift

    def greet(number, carry):
        pltpu.make_async_copy(guests.at[number], stage.at[number], sem).start()
        return carry

    lax.fori_loop(0, shift, greet, 0)

    def fetch(slot, number):
        @pl.when(number < stop)
        def _():
            pltpu.make_async_copy(strips.at[slot], stage.at[number + shift], sem).start()

    count = find_wanted(spot, tables, strips, table, sem_table, named, fetch)
    finish_blocks(strips, stage, sem, jnp.minimum(count, stop) + shift)
    hand_over(stage, [early, late], sem_out)


def pack_spare(spot, tables, strips, guests, *refs):
    *over, stage, table, sem_table, named, sem, sem_out = refs
    lent = spot[6]

    def fetch(slot, number):
        beyond = number - ALWAYS

        @pl.when((beyond >= 0) & (beyond < LENT))
        def _():
            pltpu.make_async_copy(strips.at[slot], stage.at[beyond], sem).start()

        @pl.when(beyond >= lent)
        def _():
            at = LENT + beyond - lent
            pltpu.make_async_copy(strips.at[slot], stage.at[at], sem).start()

    count = find_wanted(spot, tables, strips, table, sem_table, named, fetch)
    beyond = jnp.maximum(count - ALWAYS, 0)
    copied = jnp.minimum(beyond, LENT) + jnp.maximum(beyond - lent, 0)
    finish_blocks(strips, stage, sem, copied)
    hand_over(stage, [guests, *over], sem_out)


def find_wanted(spot, tables, strips, table, sem_table, named, action):
    rcap = strips.shape[0] // KB
    table_copy = pltpu.make_async_copy(tables, table, sem_table)
    table_copy.start()
    table_copy.wait()
    mark_rows(places_in(table, spot[0], spot[3]), table.shape[0], named)
    return for_wanted(columns_in(table, rcap, spot[1]), named, rcap, action)


def finish_blocks(source, target, sem, count):
    def finish(number, carry):
        pltpu.make_async_copy(source.at[0], target.at[0], sem).wait()
        return carry

    lax.fori_loop(0, count, finish, 0)


def hand_over(stage, outs, sem_out):
    copies, low = [], 0
    for i, out in enumerate(outs):
        here = stage.at[pl.ds(low, out.shape[0])]
        copies.append(pltpu.make_async_copy(here, out, sem_out.at[i]))
        copies[-1].start()
        low += out.shape[0]
    for copy in copies:
        copy.wait()


def pack(kernel, counts, spot, tables, strips, *more):
    size = strips.shape[-1]
    return pl.pallas_call(
        kernel,
        out_shape=[pltpu.HBM((n, size, size), strips.dtype) for n in counts],
        grid_spec=pltpu.PrefetchScalarGridSpec(
            num_scalar_prefetch=1,
            grid=(1,),
            in_specs=[ANYWHERE] * (2 + len(more)),
            out_specs=[ANYWHERE] * len(counts),
            scratch_shapes=[
                pltpu.VMEM((sum(counts), size, size), strips.dtype),
                pltpu.SMEM(tables.shape, jnp.int32),
                pltpu.SemaphoreType.DMA,
                pltpu.SMEM((KB,), jnp.int32),
                pltpu.SemaphoreType.DMA,
                pltpu.SemaphoreType.DMA((len(counts),)),
            ],
        ),
        compiler_params=pltpu.CompilerParams(vmem_limit_bytes=LIMIT),
        cost_estimate=pl.CostEstimate(
            flops=0, bytes_accessed=4 * sum(counts) * size * size, transcendentals=0
        ),
    )(spot, tables, in_hbm(strips), *more)


def after(value, blocks):
    count = len(blocks)
    return pl.pallas_call(
        lambda *refs: None,
        out_shape=[pltpu.HBM(each.shape, each.dtype) for each in blocks],
        in_specs=[ANYWHERE] * (count + 1),
        out_specs=[ANYWHERE] * count,
        input_output_aliases={i: i for i in range(count)},
        compiler_params=pltpu.CompilerParams(vmem_limit_bytes=LIMIT),
    )(*blocks, value)


def by_block_row(place, slots, order, first):
    def reset(i, carry):
        first[i] = 0
        return carry

    def count(s, carry):
        here = place(s)

        @pl.when(here >= 0)
        def _():
            i = here // KB + 2
            first[i] = first[i] + 1

        return carry

    def scan(i, carry):
        first[i] = first[i] + first[i - 1]
        return carry

    def sort(s, carry):
        here = place(s)

        @pl.when(here >= 0)
        def _():
            i = here // KB + 1
            order[first[i]] = s * KB + here % KB
            first[i] = first[i] + 1

        return carry

    lax.fori_loop(0, RB + 2, reset, 0)
    lax.fori_loop(0, slots, count, 0)
    lax.fori_loop(1, RB + 2, scan, 0)
    lax.fori_loop(0, slots, sort, 0)


def clear(right, wanted):
    def one(j, carry):
        @pl.when(wanted(j))
        def _():
            right[j] = jnp.zeros(right.shape[1:], right.dtype)

        return carry

    lax.fori_loop(0, KB, one, 0)


def add_product(total, left, right, pair):
    slot, column = pair // KB, pair % KB
    wide = right.shape[-1]
    step = 2 * left.shape[-1]
    for low in range(0, wide, step):
        here = pl.ds(low, step)
        total[:, here] += jnp.dot(
            left[slot], right[column, :, here], preferred_element_type=jnp.float32
        )


def add_rows(left, right, total, order, first):
    size = left.shape[1]

    def one_row(i, carry):
        row = pl.program_id(0) * GROUP + i
        here = pl.ds(pl.multiple_of(i * size, size), size)

        def add(entry, carry):
            add_product(total.at[here], left, right, order[entry])
            return carry

        return lax.fori_loop(first[row], first[row + 1], add, carry)

    lax.fori_loop(0, GROUP, one_row, 0)


def place_at(right, where):
    size = right.shape[1]
    start = pl.multiple_of((where % NJ) * size, size)
    return right.at[where // NJ, :, pl.ds(start, size)]


def finish_right(source, right, sem, count):
    def finish(number, carry):
        pltpu.make_async_copy(source, place_at(right, 0), sem).wait()
        return carry

    lax.fori_loop(0, count, finish, 0)


def first_kernel(
    rcap, spot, tables, received, strips,
    out, next_order, next_first, next_target,
    left, right, table, sem_table, order, first, named, other, sem_left, sem_right,
):
    slots, size, _ = left.shape

    @pl.when(pl.program_id(0) == 0)
    def _():
        left_copy = pltpu.make_async_copy(received, left, sem_left)
        left_copy.start()
        table_copy = pltpu.make_async_copy(tables, table, sem_table)
        table_copy.start()
        table_copy.wait()
        place = places_in(table, 0, spot[1])
        column = columns_in(table, rcap, spot[1])
        mark_rows(place, slots, named)
        clear(right, lambda j: named[j] > 0)

        def fetch(slot, number):
            target = place_at(right, slot // rcap * NJ + column(slot))
            pltpu.make_async_copy(strips.at[slot], target, sem_right).start()

        count = for_wanted(column, named, rcap, fetch)
        by_block_row(place, slots, order, first)

        next_place = places_in(table, spot[0], spot[2])
        next_column = columns_in(table, rcap, spot[4])
        by_block_row(next_place, slots, next_order, next_first)
        mark_rows(next_place, slots, other)

        def note(slot, number):
            next_target[number] = slot // rcap * NJ + next_column(slot)

        next_first[RB + 2] = for_wanted(next_column, other, rcap, note)
        left_copy.wait()
        finish_right(strips.at[0], right, sem_right, count)

    out[...] = jnp.zeros(out.shape, out.dtype)
    add_rows(left, right, out, order, first)


def start_left(shifted, parts, left, on_last, sem):
    step = left.shape[1] // len(parts)
    whole = pltpu.make_async_copy(shifted, left, sem)

    @pl.when(on_last)
    def _():
        for q, part in enumerate(parts):
            pltpu.make_async_copy(part, left.at[:, pl.ds(q * step, step)], sem).start()

    @pl.when(jnp.logical_not(on_last))
    def _():
        whole.start()

    return whole


def start_right(sources, count, target, right, sem):
    for blocks, low, start, stop in sources:

        def fetch(number, carry):
            pltpu.make_async_copy(
                blocks.at[number - low], place_at(right, target[number]), sem
            ).start()
            return carry

        lax.fori_loop(start, jnp.minimum(count, stop), fetch, 0)


def add_products(row, order, first, left, right, touched, total):
    def add(entry, carry):
        @pl.when(touched[order[entry] % KB] > 0)
        def _():
            add_product(total.at[row], left, right, order[entry])

        return carry

    lax.fori_loop(first[row], first[row + 1], add, 0)


def mark_targets(target, begin, end, marks):
    def reset(j, carry):
        marks[j] = 0
        return carry

    def mark(number, carry):
        marks[target[number] // NJ] = 1
        return carry

    lax.fori_loop(0, KB, reset, 0)
    lax.fori_loop(begin, end, mark, 0)


def mark_open(order, first, touched, open_row):
    def one(row, carry):
        def look(entry, found):
            return jnp.maximum(found, touched[order[entry] % KB])

        open_row[row] = lax.fori_loop(first[row], first[row + 1], look, jnp.int32(0))
        return carry

    lax.fori_loop(0, RB, one, 0)


def strip_of(ref, row, size):
    return ref.at[pl.ds(pl.multiple_of(row * size, size), size)]


def middle_kernel(parts_count, order, first, target, flags, *refs):
    shifted, *parts = refs[: 1 + parts_count]
    (
        piece, prev, out, rounded, guests, later, open_row,
        hall, sem_in, sem_home,
        left, right, total, short, touched,
        sem_left, sem_right, sem_prev, sem_out,
    ) = refs[1 + parts_count :]
    arrive = pltpu.make_async_copy(piece.at[pl.ds(0, LENT)], hall, sem_in)
    leave = pltpu.make_async_copy(hall, guests, sem_home)
    arrive.start()
    size = left.shape[1]
    count = first[RB + 2]
    shift = flags[1]
    end = piece.shape[0] - shift

    def prev_copy(row):
        return pltpu.make_async_copy(strip_of(prev, row, size), total.at[row], sem_prev.at[row])

    def start_prev(row, carry):
        prev_copy(row).start()
        return carry

    lax.fori_loop(0, RB, start_prev, 0)
    whole = start_left(shifted, parts, left, flags[0] > 0, sem_left)
    fetched = jnp.minimum(count, end)
    mark_targets(target, 0, fetched, touched)
    clear(right, lambda j: touched[j] > 0)
    start_right([(piece, -shift, 0, end)], fetched, target, right, sem_right)
    arrive.wait()
    leave.start()
    mark_targets(target, end, count, later)
    mark_open(order, first, later, open_row)
    whole.wait()
    finish_right(piece.at[0], right, sem_right, fetched)

    def out_copies(row):
        return (
            pltpu.make_async_copy(total.at[row], strip_of(out, row, size), sem_out.at[row]),
            pltpu.make_async_copy(short.at[row], strip_of(rounded, row, size), sem_out.at[row]),
        )

    def one_row(row, carry):
        open_copy, closed_copy = out_copies(row)
        prev_copy(row).wait()
        add_products(row, order, first, left, right, touched, total)

        @pl.when(open_row[row] > 0)
        def _():
            open_copy.start()

        @pl.when(open_row[row] == 0)
        def _():
            short[row] = total[row].astype(short.dtype)
            closed_copy.start()

        return carry

    def close_row(row, carry):
        open_copy, closed_copy = out_copies(row)

        @pl.when(open_row[row] > 0)
        def _():
            open_copy.wait()

        @pl.when(open_row[row] == 0)
        def _():
            closed_copy.wait()

        return carry

    lax.fori_loop(0, RB, one_row, 0)
    lax.fori_loop(0, RB, close_row, 0)
    leave.wait()


def last_kernel(parts_count, order, first, target, flags, touched, open_row, *refs):
    shifted, *parts = refs[: 1 + parts_count]
    (
        piece, back, *over, prev, _, out,
        left, right, total, short,
        sem_left, sem_right, sem_prev, sem_out,
    ) = refs[1 + parts_count :]
    size = left.shape[1]
    count = first[RB + 2]
    shift, lent = flags[1], flags[2]
    begin = PARTS[0] - shift

    def prev_copy(row):
        return pltpu.make_async_copy(strip_of(prev, row, size), total.at[row], sem_prev.at[row])

    def start_prev(row, carry):
        @pl.when(open_row[row] > 0)
        def _():
            prev_copy(row).start()

        return carry

    lax.fori_loop(0, RB, start_prev, 0)
    whole = start_left(shifted, parts, left, flags[0] > 0, sem_left)
    low = ALWAYS
    sources = [(piece, begin, begin, low - shift), (back, low, low, low + lent)]
    low = low + lent
    for blocks in over:
        high = low + blocks.shape[0]
        sources.append((blocks, low, low, high))
        low = high
    clear(right, lambda j: touched[j] > 0)
    start_right(sources, count, target, right, sem_right)

    def out_copy(row):
        return pltpu.make_async_copy(short.at[row], strip_of(out, row, size), sem_out.at[row])

    whole.wait()
    finish_right(piece.at[0], right, sem_right, count - begin)

    def one_row(row, carry):
        @pl.when(open_row[row] > 0)
        def _():
            prev_copy(row).wait()
            add_products(row, order, first, left, right, touched, total)
            short[row] = total[row].astype(short.dtype)
            out_copy(row).start()

        return carry

    def close_row(row, carry):
        @pl.when(open_row[row] > 0)
        def _():
            out_copy(row).wait()

        return carry

    lax.fori_loop(0, RB, one_row, 0)
    lax.fori_loop(0, RB, close_row, 0)


def step_call(kernel, scalars, operands, specs, out_shape, out_specs, scratch, slots, size):
    return pl.pallas_call(
        kernel,
        out_shape=out_shape,
        grid_spec=pltpu.PrefetchScalarGridSpec(
            num_scalar_prefetch=len(scalars),
            grid=(RB // GROUP,),
            in_specs=specs,
            out_specs=out_specs,
            scratch_shapes=[
                pltpu.VMEM((slots, size, size), jnp.bfloat16),
                pltpu.VMEM((KB, size, NJ * size), jnp.bfloat16),
                *scratch,
                pltpu.SemaphoreType.DMA,
                pltpu.SemaphoreType.DMA,
            ],
        ),
        compiler_params=pltpu.CompilerParams(
            dimension_semantics=("arbitrary",), vmem_limit_bytes=LIMIT
        ),
        cost_estimate=pl.CostEstimate(
            flops=2 * 24 * NJ * size * size * size,
            bytes_accessed=16 * 1024 * 1024,
            transcendentals=0,
        ),
    )(*scalars, *operands)


def first_news_kernel(where_ref, cols_ref, send, out, where, cols, blocks, tile, sems):
    copies = [
        pltpu.make_async_copy(where_ref, where, sems.at[0]),
        pltpu.make_async_copy(cols_ref, cols, sems.at[1]),
    ]
    devices, count = where.shape[-1], blocks.shape[0]
    shares = devices // count
    step = blocks.shape[1] // shares
    for row in range(count):
        copies.append(
            pltpu.make_async_copy(send.at[1, 0, row * shares], blocks.at[row], sems.at[2 + row])
        )
    for copy in copies:
        copy.start()
    rcap, across = cols.shape
    tile[...] = jnp.zeros(tile.shape, tile.dtype)
    for copy in copies:
        copy.wait()
    for slot in range(rcap):
        tile[pl.ds(0, 1), pl.ds(slot * across, across)] = cols[pl.ds(slot, 1), :]
    for half in range(2):
        row, lane = divmod(half * devices, 128)
        tile[pl.ds(1 + row, 1), pl.ds(lane, devices)] = where[half]
    table = tile[...].astype(jnp.float32).astype(out.dtype)

    def fill(device, carry):
        share = pl.multiple_of(device % shares * step, step)
        out[device, pl.ds(0, step), :] = blocks[device // shares, pl.ds(share, step), :]
        out[device, pl.ds(step, 16), :] = table
        return carry

    lax.fori_loop(0, devices, fill, 0)


def first_news(where, cols, send, rows_count):
    devices = where.shape[-1]
    size = send.shape[-1]
    step = size * rows_count // devices
    return pl.pallas_call(
        first_news_kernel,
        out_shape=jax.ShapeDtypeStruct((devices, step + 16, size), send.dtype),
        in_specs=[ANYWHERE] * 3,
        scratch_shapes=[
            pltpu.VMEM(where.shape, jnp.int32),
            pltpu.VMEM(cols.shape, jnp.int32),
            pltpu.VMEM((rows_count, size, size), send.dtype),
            pltpu.VMEM((16, size), jnp.int32),
            pltpu.SemaphoreType.DMA((2 + rows_count,)),
        ],
        compiler_params=pltpu.CompilerParams(vmem_limit_bytes=LIMIT),
    )(in_hbm(where), in_hbm(cols), in_hbm(send))


def needed(where_all, cols_all, rows_count, cols_count):
    grid = where_all.reshape(-1, 2, rows_count, cols_count)
    after = jnp.concatenate([grid[:, 0, :, 1:], grid[:, 1, :, :1]], axis=-1)
    columns = jnp.arange(KB, dtype=jnp.int32)
    hit = (after[..., None] >= 0) & (after[..., None] % KB == columns)
    wanted = jnp.any(hit, axis=0).astype(jnp.int32)
    counts = jnp.sum((cols_all >= 0).astype(jnp.int32), axis=1)
    counts = jnp.roll(counts.reshape(rows_count, cols_count, KB), -1, axis=0)
    return jnp.sum(wanted * counts, axis=-1)


def swapped(value):
    return lax.ppermute(value, "col", [(i, i ^ 1) for i in range(lax.axis_size("col"))])


def local(a_send, a_where, b_strips, b_cols):
    size = a_send.shape[-1]
    rows_count = lax.axis_size("row")
    cols_count = lax.axis_size("col")
    devices = rows_count * cols_count
    both = ("row", "col")
    row_index = lax.axis_index("row")
    col_index = lax.axis_index("col")
    rcap = b_strips.shape[3]
    last = cols_count - 1

    by_slot = jnp.swapaxes(b_cols, 2, 3).reshape(rcap, KB)
    news = lax.all_to_all(
        first_news(a_where, by_slot, a_send, rows_count),
        both, split_axis=0, concat_axis=0, tiled=True,
    )
    step = size // cols_count
    part = news[:, :step]
    tables = news[:, step : step + 1 + -(-2 * devices // 128)].astype(jnp.int32)
    after_col = (col_index + 1) % cols_count
    after_half = (col_index + 1) // cols_count
    row_before = (row_index + rows_count - 1) % rows_count
    row_after = (row_index + 1) % rows_count
    needs = needed(
        tables[:, 1:].reshape(devices, -1)[:, : 2 * devices],
        tables[:, 0].reshape(devices, rcap, KB), rows_count, cols_count,
    )
    room = ALWAYS - jnp.flip(needs.reshape(rows_count, -1, 2), -1).reshape(needs.shape)
    lent = jnp.maximum(jnp.minimum(jnp.minimum(needs - ALWAYS, room), LENT), 0)
    most = jnp.max(needs - lent)

    def lent_to(row, col):
        return lax.dynamic_slice(lent, (row, col), (1, 1))[0, 0]

    spot = jnp.stack([
        after_half,
        row_index * cols_count + col_index,
        row_index * cols_count + after_col,
        row_before * cols_count + after_col,
        row_after * cols_count + col_index,
        lent_to(row_before, col_index ^ 1),
        lent_to(row_before, col_index),
    ]).astype(jnp.int32)

    received = lax.all_to_all(a_send[0, 0], both, split_axis=0, concat_axis=0, tiled=True)

    def to_row_before(blocks):
        return lax.ppermute(
            blocks, "row", [(i, (i - 1) % rows_count) for i in range(rows_count)]
        )

    strips = b_strips.reshape(KB * rcap, size, size)
    guests, *over = pack(pack_spare, (LENT, *PARTS[2:]), spot, tables, strips)
    begin, extra = ALWAYS, []
    for blocks in over:
        extra.append(lax.cond(most > begin, to_row_before, lambda same: same, blocks))
        begin += blocks.shape[0]
    early, late = pack(
        pack_main, PARTS[:2], spot, tables, strips, swapped(guests),
        *(blocks[0, :16] for blocks in extra),
    )
    early, late = map(to_row_before, after(received, [early, late]))

    shifted = lax.ppermute(received, "col", [(i + 1, i) for i in range(last)])
    (part,) = after(guests, [part])
    parts = [lax.ppermute(part, "col", [(i, last)]) for i in range(last)] + [part]

    wide = NJ * size
    strip = pl.BlockSpec((GROUP * size, wide), lambda i, *_: (i, 0))
    begun, order, first, target = step_call(
        functools.partial(first_kernel, rcap),
        (spot,), (tables, received, in_hbm(strips)), [ANYWHERE, ANYWHERE, ANYWHERE],
        [
            pltpu.HBM((RB * size, wide), jnp.float32),
            jax.ShapeDtypeStruct((devices,), jnp.int32),
            jax.ShapeDtypeStruct((RB + 3,), jnp.int32),
            jax.ShapeDtypeStruct((KB * rcap,), jnp.int32),
        ],
        [strip, IN_SMEM, IN_SMEM, IN_SMEM],
        [
            pltpu.SMEM(tables.shape, jnp.int32),
            pltpu.SemaphoreType.DMA,
            pltpu.SMEM((devices,), jnp.int32),
            pltpu.SMEM((RB + 2,), jnp.int32),
            pltpu.SMEM((KB,), jnp.int32),
            pltpu.SMEM((KB,), jnp.int32),
        ],
        devices, size,
    )

    on_last = (col_index == last).astype(jnp.int32)
    lent_here = [lent_to(row_index, col_index ^ 1), lent_to(row_index, col_index)]
    scalars = (order, first, target, jnp.stack([on_last, *lent_here]))
    lefts = (shifted, *parts)

    def finish_call(kernel, scalars, operands, out_shape, out_specs, scratch, marks, aliases):
        return pl.pallas_call(
            kernel,
            out_shape=out_shape,
            grid_spec=pltpu.PrefetchScalarGridSpec(
                num_scalar_prefetch=len(scalars),
                grid=(1,),
                in_specs=[ANYWHERE] * len(operands),
                out_specs=out_specs,
                scratch_shapes=[
                    *scratch,
                    pltpu.VMEM((devices, size, size), jnp.bfloat16),
                    pltpu.VMEM((KB, size, wide), jnp.bfloat16),
                    pltpu.VMEM((RB, size, wide), jnp.float32),
                    pltpu.VMEM((RB, size, wide), jnp.bfloat16),
                    *marks,
                    pltpu.SemaphoreType.DMA,
                    pltpu.SemaphoreType.DMA,
                    pltpu.SemaphoreType.DMA((RB,)),
                    pltpu.SemaphoreType.DMA((RB,)),
                ],
            ),
            input_output_aliases=aliases,
            compiler_params=pltpu.CompilerParams(vmem_limit_bytes=LIMIT),
            cost_estimate=pl.CostEstimate(
                flops=2 * 16 * NJ * size * size * size,
                bytes_accessed=12 * 1024 * 1024,
                transcendentals=0,
            ),
        )(*scalars, *operands)

    begun, rounded, guests, later, open_row = finish_call(
        functools.partial(middle_kernel, len(parts)), scalars,
        (*lefts, early, in_hbm(begun)),
        [
            pltpu.HBM((RB * size, wide), jnp.float32),
            pltpu.HBM((RB * size, wide), jnp.bfloat16),
            pltpu.HBM((LENT, size, size), jnp.bfloat16),
            jax.ShapeDtypeStruct((KB,), jnp.int32),
            jax.ShapeDtypeStruct((RB,), jnp.int32),
        ],
        [ANYWHERE, ANYWHERE, ANYWHERE, IN_SMEM, IN_SMEM],
        [
            pltpu.VMEM((LENT, size, size), jnp.bfloat16),
            pltpu.SemaphoreType.DMA,
            pltpu.SemaphoreType.DMA,
        ],
        [pltpu.SMEM((KB,), jnp.int32)], {},
    )
    back = swapped(guests)

    operands = (*lefts, late, back, *extra, in_hbm(begun), rounded)
    scalars = (*scalars, later, open_row)
    return finish_call(
        functools.partial(last_kernel, len(parts)), scalars, operands,
        jax.ShapeDtypeStruct((RB * size, wide), jnp.bfloat16),
        ANYWHERE, [], [], {len(scalars) + len(operands) - 1: 0},
    )


def solution(mesh):
    placed = (
        P(None, ("row", "col"), None, None, None),
        P(None, ("row", "col"), None),
        P("row", "col", None, None, None, None),
        P("row", "col", None, None),
    )
    return jax.shard_map(
        local, mesh=mesh, in_specs=placed, out_specs=P("row", "col"), check_vma=False
    )
```

profile of v0, /device:TPU:2, one launch (start us, length us, event | category | flops | bytes accessed | tf_op | source)
XLA Modules:
  0.0 122.7 jit_solution(13745724831674101117)
XLA Ops:
  0.0 2.1 %shard_map.46 = bf16[32,48,128]{2,1,0:T(8,128)(2,1)} custom-call(s32[2,1,32]{2,1,0:T(1,128)} %where_ref.1, s32[8,16]{1,0:T(8,128)} %bitcast.50, bf16[2,1,32,128,128]{4,3,2,1,0:T(8,128)(2,1)} %send.1), custom_call_target="tpu_custom_call" | custom-call | tf_op jit(solution)/shard_map/pallas_call | solution.py:580
  2.2 6.1 %all-to-all-start = ((bf16[32,48,128]{2,1,0:T(8,128)(2,1)}), bf16[32,48,128]{2,1,0:T(8,128)(2,1)S(1)}, u32[]{:S(2)}, u32[]{:S(2)}) async-start(bf16[32,48,128]{2,1,0:T(8,128)(2,1)} %shard_map.46), calls=%async_computation | async-start | bytes 786432 | tf_op jit(solution)/shard_map/all_to_all | solution.py:622
  8.3 2.3 %slice_bitcast_fusion = bf16[32,128,128]{2,1,0:T(8,128)(2,1)} fusion(bf16[2,1,32,128,128]{4,3,2,1,0:T(8,128)(2,1)} %send.1), kind=kLoop, calls=%fused_computation | loop fusion | bytes 2097152 | tf_op jit(solution)/shard_map/squeeze | solution.py:654
  10.7 9.5 %all-to-all-done = bf16[32,48,128]{2,1,0:T(8,128)(2,1)S(1)} async-done(((bf16[32,48,128]{2,1,0:T(8,128)(2,1)}), bf16[32,48,128]{2,1,0:T(8,128)(2,1)S(1)}, u32[]{:S(2)}, u32[]{:S(2)}) %all-to-all-start) | async-done | bytes 393248 | tf_op jit(solution)/shard_map/all_to_all | solution.py:622
  20.2 3.9 %all-to-all-start.1 = ((bf16[32,128,128]{2,1,0:T(8,128)(2,1)}), bf16[32,128,128]{2,1,0:T(8,128)(2,1)S(1)}, u32[]{:S(2)}, u32[]{:S(2)}) async-start(bf16[32,128,128]{2,1,0:T(8,128)(2,1)} %slice_bitcast_fusion), calls=%async_computation.1 | async-start | bytes 2097152 | tf_op jit(solution)/shard_map/all_to_all | solution.py:654
  24.2 0.1 copy.31
  24.3 0.1 copy.34
  24.4 0.1 slice.86
  24.5 0.1 copy.36
  24.6 0.1 copy.35
  24.7 0.6 fusion.1
  25.4 0.2 fusion.3
  25.6 0.1 copy.37
  25.7 0.6 subtract_reduce_fusion
  26.4 0.1 copy.38
  26.5 0.7 fusion.5
  27.1 1.3 %stack.32.spot = s32[7]{0:T(128)S(1)} concatenate(s32[1]{0:T(128)} %bitcast, s32[1]{0:T(128)} %bitcast.1, s32[1]{0:T(128)} %bitcast.2, s32[1]{0:T(128)} %bitcast.3, s32[1]{0:T(128)} %bitcast.4, s32[1]{0:T(128)} %bitcast.17, s32[1]{0:T(128)} %bitcast.18), dimensions={0} | concatenate | bytes 56 | tf_op jit(solution)/shard_map/stack | solution.py:644
  28.5 5.6 %shard_map.48 = (bf16[16,128,128]{2,1,0:T(8,128)(2,1)}, bf16[8,128,128]{2,1,0:T(8,128)(2,1)}, bf16[8,128,128]{2,1,0:T(8,128)(2,1)}, bf16[20,128,128]{2,1,0:T(8,128)(2,1)}) custom-call(s32[7]{0:T(128)S(1)} %stack.32.spot, s32[32,2,128]{2,1,0:T(2,128)S(1)} %slice_convert_fusion.tables, bf16[128,128,128]{2,1,0:T(8,128)(2,1)} %bitcast.37), custom_call_target="tpu_custom_call" | custom-call | bytes 3407872 | tf_op jit(solution)/shard_map/pallas_call | solution.py:144
  34.1 0.2 collective-permute-start.7
  36.3 0.7 slice_bitcast_fusion.4.refs_0_
  37.0 0.7 slice_bitcast_fusion.2
  37.6 0.0 collective-permute-done.7.guests
  37.6 6.7 %shard_map.50 = (bf16[66,128,128]{2,1,0:T(8,128)(2,1)}, bf16[26,128,128]{2,1,0:T(8,128)(2,1)}) custom-call(s32[7]{0:T(128)S(1)} %stack.32.spot, s32[32,2,128]{2,1,0:T(2,128)S(1)} %slice_convert_fusion.tables, bf16[128,128,128]{2,1,0:T(8,128)(2,1)} %bitcast.38, bf16[16,128,128]{2,1,0:T(8,128)(2,1)S(1)} %collective-permute-done.7.guests, ...), custom_call_target="tpu_custom_call" | custom-call | bytes 6029312 | tf_op jit(solution)/shard_map/pallas_call | solution.py:144
  44.4 5.7 %all-to-all-done.1.received.refs_2_ = bf16[32,128,128]{2,1,0:T(8,128)(2,1)S(1)} async-done(((bf16[32,128,128]{2,1,0:T(8,128)(2,1)}), bf16[32,128,128]{2,1,0:T(8,128)(2,1)S(1)}, u32[]{:S(2)}, u32[]{:S(2)}) %all-to-all-start.1) | async-done | bytes 1048608 | tf_op jit(solution)/shard_map/all_to_all | solution.py:654
  50.1 2.3 %collective-permute-start.8 = (bf16[66,128,128]{2,1,0:T(8,128)(2,1)}, bf16[66,128,128]{2,1,0:T(8,128)(2,1)}, u32[]{:S(2)}, u32[]{:S(2)}) collective-permute-start(bf16[66,128,128]{2,1,0:T(8,128)(2,1)} %get-tuple-element.64), channel_id=1, source_target_pairs={{0,28},{4,0},{8,4},{12,8},{16,12},{20,16},{24,20},{28,24},{1,29},{... | collective-permute-start | bytes 6488072 | tf_op jit(solution)/shard_map/ppermute | solution.py:657
  52.4 1.9 %collective-permute-start.3 = (bf16[32,128,128]{2,1,0:T(8,128)(2,1)S(1)}, bf16[32,128,128]{2,1,0:T(8,128)(2,1)S(1)}, u32[]{:S(2)}, u32[]{:S(2)}) collective-permute-start(bf16[32,128,128]{2,1,0:T(8,128)(2,1)S(1)} %all-to-all-done.1.received.refs_2_), channel_id=1, source_target_pairs={{1,0},{2,1},{3,2},{5,4},{6,5},{7,6},{9,8},{10,9},{11,10},{13,12},{... | collective-permute-start | bytes 3145736 | tf_op jit(solution)/shard_map/ppermute | solution.py:673
  54.3 0.7 slice.88.refs_0_
  55.1 0.0 copy-done.1
  55.1 2.6 %collective-permute-start.6 = (bf16[32,32,128]{2,1,0:T(8,128)(2,1)}, bf16[32,32,128]{2,1,0:T(8,128)(2,1)S(1)}, u32[]{:S(2)}, u32[]{:S(2)}) collective-permute-start(bf16[32,32,128]{2,1,0:T(8,128)(2,1)} %shard_map.49.refs_4_), channel_id=1, source_target_pairs={{2,3},{6,7},{10,11},{14,15},{18,19},{22,23},{26,27},{30,31}} | collective-permute-start | bytes 786440 | tf_op jit(solution)/shard_map/ppermute | solution.py:675
  57.7 0.6 collective-permute-start.9
  58.3 0.7 collective-permute-start.5
  59.0 0.0 collective-permute-done.6.refs_3_
  59.0 0.7 collective-permute-start.4
  59.7 1.3 %pad_add_fusion.1.flags = s32[3]{0:T(128)S(1)} fusion(s32[1]{0:T(128)} %bitcast.23, s32[1]{0:T(128)} %bitcast.22, s32[1]{0:T(128)} %bitcast.21), kind=kLoop, calls=%fused_computation.22 | loop fusion | flops 6 | bytes 24 | tf_op jit(solution)/shard_map/stack | solution.py:702
  61.0 20.3 %shard_map.47 = (f32[2048,1024]{1,0:T(8,128)}, s32[32]{0:T(128)S(1)}, s32[19]{0:T(128)S(1)}, s32[128]{0:T(128)S(1)}) custom-call(s32[7]{0:T(128)S(1)} %stack.32.spot, s32[32,2,128]{2,1,0:T(2,128)S(1)} %slice_convert_fusion.tables, bf16[32,128,128]{2,1,0:T(8,128)(2,1)S(1)} %all-to-all-done.1.received.refs_2_, bf16[128,128,128]{2,1,0:T(8,128)(2,1)} %bitcast.39), custom_call_target="tpu_custom_call" | custom-call | flops 805306368 | bytes 16777216 | tf_op jit(solution)/shard_map/pallas_call | solution.py:515
  81.4 0.0 collective-permute-done.5.refs_2_
  81.4 0.0 collective-permute-done.4.refs_1_
  81.4 0.0 collective-permute-done.3.refs_0_
  81.4 18.9 %collective-permute-done.8.refs_5_ = bf16[66,128,128]{2,1,0:T(8,128)(2,1)} collective-permute-done((bf16[66,128,128]{2,1,0:T(8,128)(2,1)}, bf16[66,128,128]{2,1,0:T(8,128)(2,1)}, u32[]{:S(2)}, u32[]{:S(2)}) %collective-permute-start.8) | collective-permute-done | bytes 2162720 | tf_op jit(solution)/shard_map/ppermute | solution.py:657
  100.3 0.0 copy-done
  100.3 12.0 %shard_map.52 = (f32[2048,1024]{1,0:T(8,128)}, bf16[2048,1024]{1,0:T(8,128)(2,1)}, bf16[16,128,128]{2,1,0:T(8,128)(2,1)}, s32[16]{0:T(128)S(1)}, s32[16]{0:T(128)S(1)}) custom-call(s32[32]{0:T(128)S(1)} %get-tuple-element.55.order, s32[19]{0:T(128)S(1)} %get-tuple-element.56.first, s32[128]{0:T(128)S(1)} %get-tuple-element.57.target, ...), custom_call_target="tpu_custom_call" | custom-call | flops 536870912 | bytes 12582912 | tf_op jit(solution)/shard_map/pallas_call | solution.py:706
  112.3 0.1 collective-permute-start.10
  112.4 5.1 %collective-permute-done.9.refs_5_ = bf16[26,128,128]{2,1,0:T(8,128)(2,1)} collective-permute-done((bf16[26,128,128]{2,1,0:T(8,128)(2,1)}, bf16[26,128,128]{2,1,0:T(8,128)(2,1)}, u32[]{:S(2)}, u32[]{:S(2)}) %collective-permute-start.9) | collective-permute-done | bytes 852000 | tf_op jit(solution)/shard_map/ppermute | solution.py:657
  117.5 0.0 collective-permute-done.10.refs_6_
  117.5 0.0 copy-done.2
  117.5 0.0 copy-done.3
  117.5 0.0 copy-done.4
  117.5 5.2 %shard_map.53 = bf16[2048,1024]{1,0:T(8,128)(2,1)} custom-call(s32[32]{0:T(128)S(1)} %get-tuple-element.55.order, s32[19]{0:T(128)S(1)} %get-tuple-element.56.first, s32[128]{0:T(128)S(1)} %get-tuple-element.57.target, s32[3]{0:T(128)S(1)} %pad_add_fusion.1.flags, s32[16]{0:T(128)S(1)} %get-tuple-element.66.touched, ...), custom_call_target="tpu_custom_call", output_to_operand_aliasing={{}: (17, {})} | custom-call | flops 536870912 | bytes 12582912 | tf_op jit(solution)/shard_map/pallas_call | solution.py:706
  (22 shorter events, 0.2 us)
Async XLA Ops:
  2.2 18.0 %all-to-all-start = ((bf16[32,48,128]{2,1,0:T(8,128)(2,1)}), bf16[32,48,128]{2,1,0:T(8,128)(2,1)S(1)}, u32[]{:S(2)}, u32[]{:S(2)}) async-start(bf16[32,48,128]{2,1,0:T(8,128)(2,1)} %shard_map.46), calls=%async_computation | async-start | bytes 786432 | tf_op jit(solution)/shard_map/all_to_all | solution.py:622
  20.2 29.9 %all-to-all-start.1 = ((bf16[32,128,128]{2,1,0:T(8,128)(2,1)}), bf16[32,128,128]{2,1,0:T(8,128)(2,1)S(1)}, u32[]{:S(2)}, u32[]{:S(2)}) async-start(bf16[32,128,128]{2,1,0:T(8,128)(2,1)} %slice_bitcast_fusion), calls=%async_computation.1 | async-start | bytes 2097152 | tf_op jit(solution)/shard_map/all_to_all | solution.py:654
  34.1 3.6 %collective-permute-start.7 = (bf16[16,128,128]{2,1,0:T(8,128)(2,1)}, bf16[16,128,128]{2,1,0:T(8,128)(2,1)S(1)}, u32[]{:S(2)}, u32[]{:S(2)}) collective-permute-start(bf16[16,128,128]{2,1,0:T(8,128)(2,1)} %get-tuple-element.58.refs_1_), channel_id=1, source_target_pairs={{0,1},{1,0},{2,3},{3,2},{4,5},{5,4},{6,7},{7,6},{8,9},{9,8},{10,11... | collective-permute-start | bytes 1572872 | tf_op jit(solution)/shard_map/ppermute | solution.py:607
  37.6 17.4 %copy-start.1 = (bf16[16,128,128]{2,1,0:T(8,128)(2,1)S(1)}, bf16[16,128,128]{2,1,0:T(8,128)(2,1)}, u32[]{:S(2)}) copy-start(bf16[16,128,128]{2,1,0:T(8,128)(2,1)} %get-tuple-element.58.refs_1_) | copy-start | bytes 1572868
  50.1 50.2 %collective-permute-start.8 = (bf16[66,128,128]{2,1,0:T(8,128)(2,1)}, bf16[66,128,128]{2,1,0:T(8,128)(2,1)}, u32[]{:S(2)}, u32[]{:S(2)}) collective-permute-start(bf16[66,128,128]{2,1,0:T(8,128)(2,1)} %get-tuple-element.64), channel_id=1, source_target_pairs={{0,28},{4,0},{8,4},{12,8},{16,12},{20,16},{24,20},{28,24},{1,29},{... | collective-permute-start | bytes 6488072 | tf_op jit(solution)/shard_map/ppermute | solution.py:657
  52.4 29.0 %collective-permute-start.3 = (bf16[32,128,128]{2,1,0:T(8,128)(2,1)S(1)}, bf16[32,128,128]{2,1,0:T(8,128)(2,1)S(1)}, u32[]{:S(2)}, u32[]{:S(2)}) collective-permute-start(bf16[32,128,128]{2,1,0:T(8,128)(2,1)S(1)} %all-to-all-done.1.received.refs_2_), channel_id=1, source_target_pairs={{1,0},{2,1},{3,2},{5,4},{6,5},{7,6},{9,8},{10,9},{11,10},{13,12},{... | collective-permute-start | bytes 3145736 | tf_op jit(solution)/shard_map/ppermute | solution.py:673
  55.1 45.2 %copy-start = (bf16[32,32,128]{2,1,0:T(8,128)(2,1)S(1)}, bf16[32,32,128]{2,1,0:T(8,128)(2,1)}, u32[]{:S(2)}) copy-start(bf16[32,32,128]{2,1,0:T(8,128)(2,1)} %shard_map.49.refs_4_) | copy-start | bytes 786436
  55.1 3.9 %collective-permute-start.6 = (bf16[32,32,128]{2,1,0:T(8,128)(2,1)}, bf16[32,32,128]{2,1,0:T(8,128)(2,1)S(1)}, u32[]{:S(2)}, u32[]{:S(2)}) collective-permute-start(bf16[32,32,128]{2,1,0:T(8,128)(2,1)} %shard_map.49.refs_4_), channel_id=1, source_target_pairs={{2,3},{6,7},{10,11},{14,15},{18,19},{22,23},{26,27},{30,31}} | collective-permute-start | bytes 786440 | tf_op jit(solution)/shard_map/ppermute | solution.py:675
  57.7 59.8 %collective-permute-start.9 = (bf16[26,128,128]{2,1,0:T(8,128)(2,1)}, bf16[26,128,128]{2,1,0:T(8,128)(2,1)}, u32[]{:S(2)}, u32[]{:S(2)}) collective-permute-start(bf16[26,128,128]{2,1,0:T(8,128)(2,1)} %get-tuple-element.68), channel_id=1, source_target_pairs={{0,28},{4,0},{8,4},{12,8},{16,12},{20,16},{24,20},{28,24},{1,29},{... | collective-permute-start | bytes 2555912 | tf_op jit(solution)/shard_map/ppermute | solution.py:657
  58.3 23.1 %collective-permute-start.5 = (bf16[32,32,128]{2,1,0:T(8,128)(2,1)}, bf16[32,32,128]{2,1,0:T(8,128)(2,1)S(1)}, u32[]{:S(2)}, u32[]{:S(2)}) collective-permute-start(bf16[32,32,128]{2,1,0:T(8,128)(2,1)} %shard_map.49.refs_4_), channel_id=1, source_target_pairs={{1,3},{5,7},{9,11},{13,15},{17,19},{21,23},{25,27},{29,31}} | collective-permute-start | bytes 786440 | tf_op jit(solution)/shard_map/ppermute | solution.py:675
  59.0 22.4 %collective-permute-start.4 = (bf16[32,32,128]{2,1,0:T(8,128)(2,1)}, bf16[32,32,128]{2,1,0:T(8,128)(2,1)S(1)}, u32[]{:S(2)}, u32[]{:S(2)}) collective-permute-start(bf16[32,32,128]{2,1,0:T(8,128)(2,1)} %shard_map.49.refs_4_), channel_id=1, source_target_pairs={{0,3},{4,7},{8,11},{12,15},{16,19},{20,23},{24,27},{28,31}} | collective-permute-start | bytes 786440 | tf_op jit(solution)/shard_map/ppermute | solution.py:675
  100.3 17.2 %copy-start.2 = (bf16[20,128,128]{2,1,0:T(8,128)(2,1)S(1)}, bf16[20,128,128]{2,1,0:T(8,128)(2,1)}, u32[]{:S(2)}) copy-start(bf16[20,128,128]{2,1,0:T(8,128)(2,1)} %get-tuple-element.82.refs_9_) | copy-start | bytes 1966084
  100.3 17.2 %copy-start.3 = (bf16[8,128,128]{2,1,0:T(8,128)(2,1)S(1)}, bf16[8,128,128]{2,1,0:T(8,128)(2,1)}, u32[]{:S(2)}) copy-start(bf16[8,128,128]{2,1,0:T(8,128)(2,1)} %get-tuple-element.81.refs_8_) | copy-start | bytes 786436
  100.3 17.2 %copy-start.4 = (bf16[8,128,128]{2,1,0:T(8,128)(2,1)S(1)}, bf16[8,128,128]{2,1,0:T(8,128)(2,1)}, u32[]{:S(2)}) copy-start(bf16[8,128,128]{2,1,0:T(8,128)(2,1)} %get-tuple-element.80.refs_7_) | copy-start | bytes 786436
  112.3 5.2 %collective-permute-start.10 = (bf16[16,128,128]{2,1,0:T(8,128)(2,1)}, bf16[16,128,128]{2,1,0:T(8,128)(2,1)S(1)}, u32[]{:S(2)}, u32[]{:S(2)}) collective-permute-start(bf16[16,128,128]{2,1,0:T(8,128)(2,1)} %get-tuple-element.69), channel_id=1, source_target_pairs={{0,1},{1,0},{2,3},{3,2},{4,5},{5,4},{6,7},{7,6},{8,9},{9,8},{10,11... | collective-permute-start | bytes 1572872 | tf_op jit(solution)/shard_map/ppermute | solution.py:607
where the time goes:
time: 124 us; the launch traced here: 123 us
  Pallas kernels  52 us (42%)
  waiting for transfers between devices  39.3 us (32%)
  starting transfers between devices  19.1 us (15%)
  local copies, waits for them, and re-layouts  7.09 us (6%)
  other arithmetic  2.94 us (2%)
  between operations  2.24 us (2%)
    ppermute x2, waiting for transfers between devices, to_row_before(): lax.ppermute(blocks, 'row', [(i, (i - 1) % rows_count) for i in range(row...  24 us
    pallas_call x1, Pallas kernels, step_call(): pl.pallas_call(kernel, out_shape=out_shape, grid_spec=pltpu.PrefetchScala...  20.3 us
    pallas_call x2, Pallas kernels, finish_call(): pl.pallas_call(kernel, out_shape=out_shape, grid_spec=pltpu.PrefetchScala...  17.2 us
    pallas_call x2, Pallas kernels, pack(): pl.pallas_call(kernel, out_shape=[pltpu.HBM((n, size, size), strips.dtype...  12.3 us
    all_to_all x1, waiting for transfers between devices, local(): lax.all_to_all(first_news(a_where, by_slot, a_send, rows_count), both, sp...  9.52 us
    all_to_all x1, starting transfers between devices, local(): lax.all_to_all(first_news(a_where, by_slot, a_send, rows_count), both, sp...  6.13 us
    all_to_all x1, waiting for transfers between devices, local(): lax.all_to_all(a_send[0, 0], both, split_axis=0, concat_axis=0, tiled=True)  5.66 us
    ppermute x3, starting transfers between devices, local(): lax.ppermute(part, 'col', [(i, last)])  3.93 us
  transfers between devices with their start and end apart: 10, of which 4 were waited for; matrix products, arithmetic and copies ran while one was open for 8% of the time, Pallas kernels for 36%

commit v1 on v0

--- a/solution.py
+++ b/solution.py
@@ -10,7 +10,7 @@
 RB = 16
 KB = 16
 NJ = 8
-PARTS = (66, 26, 8, 8, 20)
+PARTS = (66, 24, 8, 8, 22)
 ALWAYS = PARTS[0] + PARTS[1]
 LENT = 16
 GROUP = 4
@@ -165,16 +165,16 @@
     )(spot, tables, in_hbm(strips), *more)
 
 
-def after(value, blocks):
+def after(values, blocks):
     count = len(blocks)
     return pl.pallas_call(
         lambda *refs: None,
         out_shape=[pltpu.HBM(each.shape, each.dtype) for each in blocks],
-        in_specs=[ANYWHERE] * (count + 1),
+        in_specs=[ANYWHERE] * (count + len(values)),
         out_specs=[ANYWHERE] * count,
         input_output_aliases={i: i for i in range(count)},
         compiler_params=pltpu.CompilerParams(vmem_limit_bytes=LIMIT),
-    )(*blocks, value)
+    )(*blocks, *values)
 
 
 def by_block_row(place, slots, order, first):
@@ -660,18 +660,15 @@
 
     strips = b_strips.reshape(KB * rcap, size, size)
     guests, *over = pack(pack_spare, (LENT, *PARTS[2:]), spot, tables, strips)
+    early, late = pack(pack_main, PARTS[:2], spot, tables, strips, swapped(guests))
     begin, extra = ALWAYS, []
-    for blocks in over:
+    for blocks in after([received, early], over):
         extra.append(lax.cond(most > begin, to_row_before, lambda same: same, blocks))
         begin += blocks.shape[0]
-    early, late = pack(
-        pack_main, PARTS[:2], spot, tables, strips, swapped(guests),
-        *(blocks[0, :16] for blocks in extra),
-    )
-    early, late = map(to_row_before, after(received, [early, late]))
+    early, late = map(to_row_before, after([received, *extra], [early, late]))
 
     shifted = lax.ppermute(received, "col", [(i + 1, i) for i in range(last)])
-    (part,) = after(guests, [part])
+    (part,) = after([guests], [part])
     parts = [lax.ppermute(part, "col", [(i, last)]) for i in range(last)] + [part]
 
     wide = NJ * size

time: 124 us -> 124 us (level)
  the two profiles are of different devices: /device:TPU:2 before, /device:TPU:30 now
where the time goes in v1:
time: 124 us; the launch traced here: 122 us
  Pallas kernels  47.6 us (38%)
  waiting for transfers between devices  42.2 us (34%)
  starting transfers between devices  19.7 us (16%)
  local copies, waits for them, and re-layouts  7.35 us (6%)
  other arithmetic  2.99 us (2%)
  between operations  2.24 us (2%)
    ppermute x2, waiting for transfers between devices, to_row_before(): lax.ppermute(blocks, 'row', [(i, (i - 1) % rows_count) for i in range(row...  29.4 us
    pallas_call x1, Pallas kernels, step_call(): pl.pallas_call(kernel, out_shape=out_shape, grid_spec=pltpu.PrefetchScala...  17.5 us
    pallas_call x2, Pallas kernels, finish_call(): pl.pallas_call(kernel, out_shape=out_shape, grid_spec=pltpu.PrefetchScala...  16.4 us
    pallas_call x2, Pallas kernels, pack(): pl.pallas_call(kernel, out_shape=[pltpu.HBM((n, size, size), strips.dtype...  11.6 us
    all_to_all x1, waiting for transfers between devices, local(): lax.all_to_all(first_news(a_where, by_slot, a_send, rows_count), both, sp...  7.6 us
    all_to_all x1, starting transfers between devices, local(): lax.all_to_all(a_send[0, 0], both, split_axis=0, concat_axis=0, tiled=True)  5.85 us
    all_to_all x1, starting transfers between devices, local(): lax.all_to_all(first_news(a_where, by_slot, a_send, rows_count), both, sp...  5.84 us
    all_to_all x1, waiting for transfers between devices, local(): lax.all_to_all(a_send[0, 0], both, split_axis=0, concat_axis=0, tiled=True)  5.25 us
  transfers between devices with their start and end apart: 10, of which 4 were waited for; matrix products, arithmetic and copies ran while one was open for 7% of the time, Pallas kernels for 34%

profile of v1, /device:TPU:30, one launch (start us, length us, event | category | flops | bytes accessed | tf_op | source)
XLA Modules:
  0.0 122.1 jit_solution(10932258792859285733)
XLA Ops:
  0.0 2.1 %shard_map.46 = bf16[32,48,128]{2,1,0:T(8,128)(2,1)} custom-call(s32[2,1,32]{2,1,0:T(1,128)} %where_ref.1, s32[8,16]{1,0:T(8,128)} %bitcast.44, bf16[2,1,32,128,128]{4,3,2,1,0:T(8,128)(2,1)} %send.1), custom_call_target="tpu_custom_call" | custom-call | tf_op jit(solution)/shard_map/pallas_call | solution.py:580
  2.2 5.8 %all-to-all-start = ((bf16[32,48,128]{2,1,0:T(8,128)(2,1)}), bf16[32,48,128]{2,1,0:T(8,128)(2,1)S(1)}, u32[]{:S(2)}, u32[]{:S(2)}) async-start(bf16[32,48,128]{2,1,0:T(8,128)(2,1)} %shard_map.46), calls=%async_computation | async-start | bytes 786432 | tf_op jit(solution)/shard_map/all_to_all | solution.py:622
  8.1 2.3 %slice_bitcast_fusion = bf16[32,128,128]{2,1,0:T(8,128)(2,1)} fusion(bf16[2,1,32,128,128]{4,3,2,1,0:T(8,128)(2,1)} %send.1), kind=kLoop, calls=%fused_computation | loop fusion | bytes 2097152 | tf_op jit(solution)/shard_map/squeeze | solution.py:654
  10.4 7.6 %all-to-all-done = bf16[32,48,128]{2,1,0:T(8,128)(2,1)S(1)} async-done(((bf16[32,48,128]{2,1,0:T(8,128)(2,1)}), bf16[32,48,128]{2,1,0:T(8,128)(2,1)S(1)}, u32[]{:S(2)}, u32[]{:S(2)}) %all-to-all-start) | async-done | bytes 393248 | tf_op jit(solution)/shard_map/all_to_all | solution.py:622
  18.0 5.8 %all-to-all-start.1 = ((bf16[32,128,128]{2,1,0:T(8,128)(2,1)}), bf16[32,128,128]{2,1,0:T(8,128)(2,1)S(1)}, u32[]{:S(2)}, u32[]{:S(2)}) async-start(bf16[32,128,128]{2,1,0:T(8,128)(2,1)} %slice_bitcast_fusion), calls=%async_computation.1 | async-start | bytes 2097152 | tf_op jit(solution)/shard_map/all_to_all | solution.py:654
  23.9 0.1 copy.34
  24.0 0.1 copy.37
  24.1 0.1 slice.56
  24.2 0.1 copy.39
  24.3 0.1 copy.38
  24.5 0.6 fusion.1
  25.1 0.2 fusion.3
  25.3 0.1 copy.40
  25.4 0.6 subtract_reduce_fusion
  26.1 0.1 copy.41
  26.2 0.7 fusion.5
  26.9 1.3 %stack.32.spot = s32[7]{0:T(128)S(1)} concatenate(s32[1]{0:T(128)} %bitcast, s32[1]{0:T(128)} %bitcast.1, s32[1]{0:T(128)} %bitcast.2, s32[1]{0:T(128)} %bitcast.3, s32[1]{0:T(128)} %bitcast.4, s32[1]{0:T(128)} %bitcast.17, s32[1]{0:T(128)} %bitcast.18), dimensions={0} | concatenate | bytes 56 | tf_op jit(solution)/shard_map/stack | solution.py:644
  28.2 5.3 %shard_map.48 = (bf16[16,128,128]{2,1,0:T(8,128)(2,1)}, bf16[8,128,128]{2,1,0:T(8,128)(2,1)}, bf16[8,128,128]{2,1,0:T(8,128)(2,1)}, bf16[22,128,128]{2,1,0:T(8,128)(2,1)}) custom-call(s32[7]{0:T(128)S(1)} %stack.32.spot, s32[32,2,128]{2,1,0:T(2,128)S(1)} %slice_convert_fusion.tables, bf16[128,128,128]{2,1,0:T(8,128)(2,1)} %bitcast.31), custom_call_target="tpu_custom_call" | custom-call | bytes 3538944 | tf_op jit(solution)/shard_map/pallas_call | solution.py:144
  33.4 0.9 collective-permute-start.7
  36.3 0.0 collective-permute-done.7.guests
  36.3 6.3 %shard_map.50 = (bf16[66,128,128]{2,1,0:T(8,128)(2,1)}, bf16[24,128,128]{2,1,0:T(8,128)(2,1)}) custom-call(s32[7]{0:T(128)S(1)} %stack.32.spot, s32[32,2,128]{2,1,0:T(2,128)S(1)} %slice_convert_fusion.tables, bf16[128,128,128]{2,1,0:T(8,128)(2,1)} %bitcast.32, bf16[16,128,128]{2,1,0:T(8,128)(2,1)S(1)} %collective-permute-done.7.guests), custom_call_target="tpu_custom_call" | custom-call | bytes 5898240 | tf_op jit(solution)/shard_map/pallas_call | solution.py:144
  42.6 5.2 %all-to-all-done.1.received.refs_3_.refs_2_ = bf16[32,128,128]{2,1,0:T(8,128)(2,1)S(1)} async-done(((bf16[32,128,128]{2,1,0:T(8,128)(2,1)}), bf16[32,128,128]{2,1,0:T(8,128)(2,1)S(1)}, u32[]{:S(2)}, u32[]{:S(2)}) %all-to-all-start.1) | async-done | bytes 1048608 | tf_op jit(solution)/shard_map/all_to_all | solution.py:654
  47.9 0.0 copy-start
  47.9 1.6 %copy-done = bf16[66,128,128]{2,1,0:T(8,128)(2,1)S(1)} copy-done((bf16[66,128,128]{2,1,0:T(8,128)(2,1)S(1)}, bf16[66,128,128]{2,1,0:T(8,128)(2,1)}, u32[]{:S(2)}) %copy-start) | copy-done | bytes 2162712
  49.5 0.6 collective-permute-start.8
  50.0 1.9 %collective-permute-start.3 = (bf16[32,128,128]{2,1,0:T(8,128)(2,1)S(1)}, bf16[32,128,128]{2,1,0:T(8,128)(2,1)S(1)}, u32[]{:S(2)}, u32[]{:S(2)}) collective-permute-start(bf16[32,128,128]{2,1,0:T(8,128)(2,1)S(1)} %all-to-all-done.1.received.refs_3_.refs_2_), channel_id=1, source_target_pairs={{1,0},{2,1},{3,2},{5,4},{6,5},{7,6},{9,8},{10,9},{11,10},{13,12},{... | collective-permute-start | bytes 3145736 | tf_op jit(solution)/shard_map/ppermute | solution.py:670
  52.0 0.7 slice.58.refs_0_
  52.7 0.0 copy-done.2
  52.7 2.6 %collective-permute-start.6 = (bf16[32,32,128]{2,1,0:T(8,128)(2,1)}, bf16[32,32,128]{2,1,0:T(8,128)(2,1)S(1)}, u32[]{:S(2)}, u32[]{:S(2)}) collective-permute-start(bf16[32,32,128]{2,1,0:T(8,128)(2,1)} %shard_map.49.refs_4_), channel_id=1, source_target_pairs={{2,3},{6,7},{10,11},{14,15},{18,19},{22,23},{26,27},{30,31}} | collective-permute-start | bytes 786440 | tf_op jit(solution)/shard_map/ppermute | solution.py:672
  55.3 0.7 collective-permute-start.5
  56.0 0.7 collective-permute-start.4
  56.7 0.0 collective-permute-done.6.refs_3_
  56.7 0.6 collective-permute-start.9
  57.3 1.4 %pad_add_fusion.1.flags = s32[3]{0:T(128)S(1)} fusion(s32[1]{0:T(128)} %bitcast.23, s32[1]{0:T(128)} %bitcast.22, s32[1]{0:T(128)} %bitcast.21), kind=kLoop, calls=%fused_computation.19 | loop fusion | flops 6 | bytes 24 | tf_op jit(solution)/shard_map/stack | solution.py:699
  58.7 17.5 %shard_map.47 = (f32[2048,1024]{1,0:T(8,128)}, s32[32]{0:T(128)S(1)}, s32[19]{0:T(128)S(1)}, s32[128]{0:T(128)S(1)}) custom-call(s32[7]{0:T(128)S(1)} %stack.32.spot, s32[32,2,128]{2,1,0:T(2,128)S(1)} %slice_convert_fusion.tables, bf16[32,128,128]{2,1,0:T(8,128)(2,1)S(1)} %all-to-all-done.1.received.refs_3_.refs_2_, bf16[128,128,128]{2,1,0:T(8,128)(2,1)} %bitcast.33), custom_call_target="tpu_custom_call" | custom-call | flops 805306368 | bytes 16777216 | tf_op jit(solution)/shard_map/pallas_call | solution.py:515
  76.3 0.0 collective-permute-done.5.refs_2_
  76.3 0.0 collective-permute-done.4.refs_1_
  76.3 0.0 collective-permute-done.3.refs_0_
  76.3 26.1 %collective-permute-done.8.refs_5_ = bf16[66,128,128]{2,1,0:T(8,128)(2,1)} collective-permute-done((bf16[66,128,128]{2,1,0:T(8,128)(2,1)}, bf16[66,128,128]{2,1,0:T(8,128)(2,1)}, u32[]{:S(2)}, u32[]{:S(2)}) %collective-permute-start.8) | collective-permute-done | bytes 2162720 | tf_op jit(solution)/shard_map/ppermute | solution.py:657
  102.4 0.0 copy-done.1
  102.4 12.6 %shard_map.53 = (f32[2048,1024]{1,0:T(8,128)}, bf16[2048,1024]{1,0:T(8,128)(2,1)}, bf16[16,128,128]{2,1,0:T(8,128)(2,1)}, s32[16]{0:T(128)S(1)}, s32[16]{0:T(128)S(1)}) custom-call(s32[32]{0:T(128)S(1)} %get-tuple-element.40.order, s32[19]{0:T(128)S(1)} %get-tuple-element.41.first, s32[128]{0:T(128)S(1)} %get-tuple-element.42.target, ...), custom_call_target="tpu_custom_call" | custom-call | flops 536870912 | bytes 12582912 | tf_op jit(solution)/shard_map/pallas_call | solution.py:703
  115.0 0.1 collective-permute-start.10
  115.1 3.3 %collective-permute-done.9.refs_5_ = bf16[24,128,128]{2,1,0:T(8,128)(2,1)} collective-permute-done((bf16[24,128,128]{2,1,0:T(8,128)(2,1)}, bf16[24,128,128]{2,1,0:T(8,128)(2,1)}, u32[]{:S(2)}, u32[]{:S(2)}) %collective-permute-start.9) | collective-permute-done | bytes 786464 | tf_op jit(solution)/shard_map/ppermute | solution.py:657
  118.3 0.0 collective-permute-done.10.refs_6_
  118.3 0.0 copy-done.3
  118.3 0.0 copy-done.4
  118.4 0.0 copy-done.5
  118.4 3.8 %shard_map.54 = bf16[2048,1024]{1,0:T(8,128)(2,1)} custom-call(s32[32]{0:T(128)S(1)} %get-tuple-element.40.order, s32[19]{0:T(128)S(1)} %get-tuple-element.41.first, s32[128]{0:T(128)S(1)} %get-tuple-element.42.target, s32[3]{0:T(128)S(1)} %pad_add_fusion.1.flags, s32[16]{0:T(128)S(1)} %get-tuple-element.54.touched, ...), custom_call_target="tpu_custom_call", output_to_operand_aliasing={{}: (17, {})} | custom-call | flops 536870912 | bytes 12582912 | tf_op jit(solution)/shard_map/pallas_call | solution.py:703
  (23 shorter events, 0.2 us)
Async XLA Ops:
  2.2 15.8 %all-to-all-start = ((bf16[32,48,128]{2,1,0:T(8,128)(2,1)}), bf16[32,48,128]{2,1,0:T(8,128)(2,1)S(1)}, u32[]{:S(2)}, u32[]{:S(2)}) async-start(bf16[32,48,128]{2,1,0:T(8,128)(2,1)} %shard_map.46), calls=%async_computation | async-start | bytes 786432 | tf_op jit(solution)/shard_map/all_to_all | solution.py:622
  18.0 29.9 %all-to-all-start.1 = ((bf16[32,128,128]{2,1,0:T(8,128)(2,1)}), bf16[32,128,128]{2,1,0:T(8,128)(2,1)S(1)}, u32[]{:S(2)}, u32[]{:S(2)}) async-start(bf16[32,128,128]{2,1,0:T(8,128)(2,1)} %slice_bitcast_fusion), calls=%async_computation.1 | async-start | bytes 2097152 | tf_op jit(solution)/shard_map/all_to_all | solution.py:654
  33.4 2.8 %collective-permute-start.7 = (bf16[16,128,128]{2,1,0:T(8,128)(2,1)}, bf16[16,128,128]{2,1,0:T(8,128)(2,1)S(1)}, u32[]{:S(2)}, u32[]{:S(2)}) collective-permute-start(bf16[16,128,128]{2,1,0:T(8,128)(2,1)} %get-tuple-element.43.refs_1_), channel_id=1, source_target_pairs={{0,1},{1,0},{2,3},{3,2},{4,5},{5,4},{6,7},{7,6},{8,9},{9,8},{10,11... | collective-permute-start | bytes 1572872 | tf_op jit(solution)/shard_map/ppermute | solution.py:607
  47.9 1.6 %copy-start = (bf16[66,128,128]{2,1,0:T(8,128)(2,1)S(1)}, bf16[66,128,128]{2,1,0:T(8,128)(2,1)}, u32[]{:S(2)}) copy-start(bf16[66,128,128]{2,1,0:T(8,128)(2,1)} %get-tuple-element.44.refs_4_.refs_0_) | copy-start | bytes 6488068
  49.5 3.2 %copy-start.2 = (bf16[16,128,128]{2,1,0:T(8,128)(2,1)S(1)}, bf16[16,128,128]{2,1,0:T(8,128)(2,1)}, u32[]{:S(2)}) copy-start(bf16[16,128,128]{2,1,0:T(8,128)(2,1)} %get-tuple-element.43.refs_1_) | copy-start | bytes 1572868
  49.5 52.9 %collective-permute-start.8 = (bf16[66,128,128]{2,1,0:T(8,128)(2,1)}, bf16[66,128,128]{2,1,0:T(8,128)(2,1)}, u32[]{:S(2)}, u32[]{:S(2)}) collective-permute-start(bf16[66,128,128]{2,1,0:T(8,128)(2,1)} %get-tuple-element.52), channel_id=1, source_target_pairs={{0,28},{4,0},{8,4},{12,8},{16,12},{20,16},{24,20},{28,24},{1,29},{... | collective-permute-start | bytes 6488072 | tf_op jit(solution)/shard_map/ppermute | solution.py:657
  50.0 26.3 %collective-permute-start.3 = (bf16[32,128,128]{2,1,0:T(8,128)(2,1)S(1)}, bf16[32,128,128]{2,1,0:T(8,128)(2,1)S(1)}, u32[]{:S(2)}, u32[]{:S(2)}) collective-permute-start(bf16[32,128,128]{2,1,0:T(8,128)(2,1)S(1)} %all-to-all-done.1.received.refs_3_.refs_2_), channel_id=1, source_target_pairs={{1,0},{2,1},{3,2},{5,4},{6,5},{7,6},{9,8},{10,9},{11,10},{13,12},{... | collective-permute-start | bytes 3145736 | tf_op jit(solution)/shard_map/ppermute | solution.py:670
  52.7 49.7 %copy-start.1 = (bf16[32,32,128]{2,1,0:T(8,128)(2,1)S(1)}, bf16[32,32,128]{2,1,0:T(8,128)(2,1)}, u32[]{:S(2)}) copy-start(bf16[32,32,128]{2,1,0:T(8,128)(2,1)} %shard_map.49.refs_4_) | copy-start | bytes 786436
  52.7 4.0 %collective-permute-start.6 = (bf16[32,32,128]{2,1,0:T(8,128)(2,1)}, bf16[32,32,128]{2,1,0:T(8,128)(2,1)S(1)}, u32[]{:S(2)}, u32[]{:S(2)}) collective-permute-start(bf16[32,32,128]{2,1,0:T(8,128)(2,1)} %shard_map.49.refs_4_), channel_id=1, source_target_pairs={{2,3},{6,7},{10,11},{14,15},{18,19},{22,23},{26,27},{30,31}} | collective-permute-start | bytes 786440 | tf_op jit(solution)/shard_map/ppermute | solution.py:672
  55.3 21.0 %collective-permute-start.5 = (bf16[32,32,128]{2,1,0:T(8,128)(2,1)}, bf16[32,32,128]{2,1,0:T(8,128)(2,1)S(1)}, u32[]{:S(2)}, u32[]{:S(2)}) collective-permute-start(bf16[32,32,128]{2,1,0:T(8,128)(2,1)} %shard_map.49.refs_4_), channel_id=1, source_target_pairs={{1,3},{5,7},{9,11},{13,15},{17,19},{21,23},{25,27},{29,31}} | collective-permute-start | bytes 786440 | tf_op jit(solution)/shard_map/ppermute | solution.py:672
  56.0 20.3 %collective-permute-start.4 = (bf16[32,32,128]{2,1,0:T(8,128)(2,1)}, bf16[32,32,128]{2,1,0:T(8,128)(2,1)S(1)}, u32[]{:S(2)}, u32[]{:S(2)}) collective-permute-start(bf16[32,32,128]{2,1,0:T(8,128)(2,1)} %shard_map.49.refs_4_), channel_id=1, source_target_pairs={{0,3},{4,7},{8,11},{12,15},{16,19},{20,23},{24,27},{28,31}} | collective-permute-start | bytes 786440 | tf_op jit(solution)/shard_map/ppermute | solution.py:672
  56.7 61.7 %collective-permute-start.9 = (bf16[24,128,128]{2,1,0:T(8,128)(2,1)}, bf16[24,128,128]{2,1,0:T(8,128)(2,1)}, u32[]{:S(2)}, u32[]{:S(2)}) collective-permute-start(bf16[24,128,128]{2,1,0:T(8,128)(2,1)} %get-tuple-element.56), channel_id=1, source_target_pairs={{0,28},{4,0},{8,4},{12,8},{16,12},{20,16},{24,20},{28,24},{1,29},{... | collective-permute-start | bytes 2359304 | tf_op jit(solution)/shard_map/ppermute | solution.py:657
  102.4 16.0 %copy-start.3 = (bf16[22,128,128]{2,1,0:T(8,128)(2,1)S(1)}, bf16[22,128,128]{2,1,0:T(8,128)(2,1)}, u32[]{:S(2)}) copy-start(bf16[22,128,128]{2,1,0:T(8,128)(2,1)} %get-tuple-element.68.refs_5_.refs_9_) | copy-start | bytes 2162692
  102.4 16.0 %copy-start.4 = (bf16[8,128,128]{2,1,0:T(8,128)(2,1)S(1)}, bf16[8,128,128]{2,1,0:T(8,128)(2,1)}, u32[]{:S(2)}) copy-start(bf16[8,128,128]{2,1,0:T(8,128)(2,1)} %get-tuple-element.66.refs_3_.refs_7_) | copy-start | bytes 786436
  102.4 16.0 %copy-start.5 = (bf16[8,128,128]{2,1,0:T(8,128)(2,1)S(1)}, bf16[8,128,128]{2,1,0:T(8,128)(2,1)}, u32[]{:S(2)}) copy-start(bf16[8,128,128]{2,1,0:T(8,128)(2,1)} %get-tuple-element.67.refs_4_.refs_8_) | copy-start | bytes 786436
  115.0 3.4 %collective-permute-start.10 = (bf16[16,128,128]{2,1,0:T(8,128)(2,1)}, bf16[16,128,128]{2,1,0:T(8,128)(2,1)S(1)}, u32[]{:S(2)}, u32[]{:S(2)}) collective-permute-start(bf16[16,128,128]{2,1,0:T(8,128)(2,1)} %get-tuple-element.57), channel_id=1, source_target_pairs={{0,1},{1,0},{2,3},{3,2},{4,5},{5,4},{6,7},{7,6},{8,9},{9,8},{10,11... | collective-permute-start | bytes 1572872 | tf_op jit(solution)/shard_map/ppermute | solution.py:607

commit v2 on v0

--- a/solution.py
+++ b/solution.py
@@ -10,7 +10,7 @@
 RB = 16
 KB = 16
 NJ = 8
-PARTS = (66, 26, 8, 8, 20)
+PARTS = (70, 22, 8, 8, 20)
 ALWAYS = PARTS[0] + PARTS[1]
 LENT = 16
 GROUP = 4

time: 124 us -> 123 us (level)
  the two profiles are of different devices: /device:TPU:2 before, /device:TPU:30 now
where the time goes in v2:
time: 123 us; the launch traced here: 122 us
  Pallas kernels  50 us (41%)
  waiting for transfers between devices  40.5 us (33%)
  starting transfers between devices  18.9 us (15%)
  local copies, waits for them, and re-layouts  7.08 us (6%)
  other arithmetic  2.93 us (2%)
  between operations  2.26 us (2%)
    ppermute x2, waiting for transfers between devices, to_row_before(): lax.ppermute(blocks, 'row', [(i, (i - 1) % rows_count) for i in range(row...  28.8 us
    pallas_call x1, Pallas kernels, step_call(): pl.pallas_call(kernel, out_shape=out_shape, grid_spec=pltpu.PrefetchScala...  20.7 us
    pallas_call x2, Pallas kernels, finish_call(): pl.pallas_call(kernel, out_shape=out_shape, grid_spec=pltpu.PrefetchScala...  15 us
    pallas_call x2, Pallas kernels, pack(): pl.pallas_call(kernel, out_shape=[pltpu.HBM((n, size, size), strips.dtype...  12.1 us
    all_to_all x1, waiting for transfers between devices, local(): lax.all_to_all(first_news(a_where, by_slot, a_send, rows_count), both, sp...  7.61 us
    all_to_all x1, starting transfers between devices, local(): lax.all_to_all(a_send[0, 0], both, split_axis=0, concat_axis=0, tiled=True)  5.85 us
    all_to_all x1, starting transfers between devices, local(): lax.all_to_all(first_news(a_where, by_slot, a_send, rows_count), both, sp...  5.84 us
    all_to_all x1, waiting for transfers between devices, local(): lax.all_to_all(a_send[0, 0], both, split_axis=0, concat_axis=0, tiled=True)  4.06 us
  transfers between devices with their start and end apart: 10, of which 4 were waited for; matrix products, arithmetic and copies ran while one was open for 8% of the time, Pallas kernels for 36%

profile of v2, /device:TPU:30, one launch (start us, length us, event | category | flops | bytes accessed | tf_op | source)
XLA Modules:
  0.0 121.6 jit_solution(6495927830584091869)
XLA Ops:
  0.0 2.1 %shard_map.46 = bf16[32,48,128]{2,1,0:T(8,128)(2,1)} custom-call(s32[2,1,32]{2,1,0:T(1,128)} %where_ref.1, s32[8,16]{1,0:T(8,128)} %bitcast.50, bf16[2,1,32,128,128]{4,3,2,1,0:T(8,128)(2,1)} %send.1), custom_call_target="tpu_custom_call" | custom-call | tf_op jit(solution)/shard_map/pallas_call | solution.py:580
  2.2 5.8 %all-to-all-start = ((bf16[32,48,128]{2,1,0:T(8,128)(2,1)}), bf16[32,48,128]{2,1,0:T(8,128)(2,1)S(1)}, u32[]{:S(2)}, u32[]{:S(2)}) async-start(bf16[32,48,128]{2,1,0:T(8,128)(2,1)} %shard_map.46), calls=%async_computation | async-start | bytes 786432 | tf_op jit(solution)/shard_map/all_to_all | solution.py:622
  8.1 2.3 %slice_bitcast_fusion = bf16[32,128,128]{2,1,0:T(8,128)(2,1)} fusion(bf16[2,1,32,128,128]{4,3,2,1,0:T(8,128)(2,1)} %send.1), kind=kLoop, calls=%fused_computation | loop fusion | bytes 2097152 | tf_op jit(solution)/shard_map/squeeze | solution.py:654
  10.4 7.6 %all-to-all-done = bf16[32,48,128]{2,1,0:T(8,128)(2,1)S(1)} async-done(((bf16[32,48,128]{2,1,0:T(8,128)(2,1)}), bf16[32,48,128]{2,1,0:T(8,128)(2,1)S(1)}, u32[]{:S(2)}, u32[]{:S(2)}) %all-to-all-start) | async-done | bytes 393248 | tf_op jit(solution)/shard_map/all_to_all | solution.py:622
  18.0 5.8 %all-to-all-start.1 = ((bf16[32,128,128]{2,1,0:T(8,128)(2,1)}), bf16[32,128,128]{2,1,0:T(8,128)(2,1)S(1)}, u32[]{:S(2)}, u32[]{:S(2)}) async-start(bf16[32,128,128]{2,1,0:T(8,128)(2,1)} %slice_bitcast_fusion), calls=%async_computation.1 | async-start | bytes 2097152 | tf_op jit(solution)/shard_map/all_to_all | solution.py:654
  23.9 0.1 copy.31
  24.0 0.1 copy.34
  24.1 0.1 slice.86
  24.2 0.1 copy.36
  24.3 0.1 copy.35
  24.5 0.6 fusion.1
  25.1 0.2 fusion.3
  25.3 0.1 copy.37
  25.4 0.6 subtract_reduce_fusion
  26.1 0.1 copy.38
  26.2 0.7 fusion.5
  26.8 1.3 %stack.32.spot = s32[7]{0:T(128)S(1)} concatenate(s32[1]{0:T(128)} %bitcast, s32[1]{0:T(128)} %bitcast.1, s32[1]{0:T(128)} %bitcast.2, s32[1]{0:T(128)} %bitcast.3, s32[1]{0:T(128)} %bitcast.4, s32[1]{0:T(128)} %bitcast.17, s32[1]{0:T(128)} %bitcast.18), dimensions={0} | concatenate | bytes 56 | tf_op jit(solution)/shard_map/stack | solution.py:644
  28.2 5.5 %shard_map.48 = (bf16[16,128,128]{2,1,0:T(8,128)(2,1)}, bf16[8,128,128]{2,1,0:T(8,128)(2,1)}, bf16[8,128,128]{2,1,0:T(8,128)(2,1)}, bf16[20,128,128]{2,1,0:T(8,128)(2,1)}) custom-call(s32[7]{0:T(128)S(1)} %stack.32.spot, s32[32,2,128]{2,1,0:T(2,128)S(1)} %slice_convert_fusion.tables, bf16[128,128,128]{2,1,0:T(8,128)(2,1)} %bitcast.37), custom_call_target="tpu_custom_call" | custom-call | bytes 3407872 | tf_op jit(solution)/shard_map/pallas_call | solution.py:144
  33.7 0.1 collective-permute-start.7
  35.8 0.7 slice_bitcast_fusion.4.refs_0_
  36.5 0.7 slice_bitcast_fusion.2
  37.1 0.0 collective-permute-done.7.guests
  37.2 6.6 %shard_map.50 = (bf16[70,128,128]{2,1,0:T(8,128)(2,1)}, bf16[22,128,128]{2,1,0:T(8,128)(2,1)}) custom-call(s32[7]{0:T(128)S(1)} %stack.32.spot, s32[32,2,128]{2,1,0:T(2,128)S(1)} %slice_convert_fusion.tables, bf16[128,128,128]{2,1,0:T(8,128)(2,1)} %bitcast.38, bf16[16,128,128]{2,1,0:T(8,128)(2,1)S(1)} %collective-permute-done.7.guests, ...), custom_call_target="tpu_custom_call" | custom-call | bytes 6029312 | tf_op jit(solution)/shard_map/pallas_call | solution.py:144
  43.8 4.1 %all-to-all-done.1.received.refs_2_ = bf16[32,128,128]{2,1,0:T(8,128)(2,1)S(1)} async-done(((bf16[32,128,128]{2,1,0:T(8,128)(2,1)}), bf16[32,128,128]{2,1,0:T(8,128)(2,1)S(1)}, u32[]{:S(2)}, u32[]{:S(2)}) %all-to-all-start.1) | async-done | bytes 1048608 | tf_op jit(solution)/shard_map/all_to_all | solution.py:654
  47.9 0.6 collective-permute-start.8
  48.4 1.9 %collective-permute-start.3 = (bf16[32,128,128]{2,1,0:T(8,128)(2,1)S(1)}, bf16[32,128,128]{2,1,0:T(8,128)(2,1)S(1)}, u32[]{:S(2)}, u32[]{:S(2)}) collective-permute-start(bf16[32,128,128]{2,1,0:T(8,128)(2,1)S(1)} %all-to-all-done.1.received.refs_2_), channel_id=1, source_target_pairs={{1,0},{2,1},{3,2},{5,4},{6,5},{7,6},{9,8},{10,9},{11,10},{13,12},{... | collective-permute-start | bytes 3145736 | tf_op jit(solution)/shard_map/ppermute | solution.py:673
  50.3 0.7 slice.88.refs_0_
  51.1 0.0 copy-done.1
  51.1 2.6 %collective-permute-start.6 = (bf16[32,32,128]{2,1,0:T(8,128)(2,1)}, bf16[32,32,128]{2,1,0:T(8,128)(2,1)S(1)}, u32[]{:S(2)}, u32[]{:S(2)}) collective-permute-start(bf16[32,32,128]{2,1,0:T(8,128)(2,1)} %shard_map.49.refs_4_), channel_id=1, source_target_pairs={{2,3},{6,7},{10,11},{14,15},{18,19},{22,23},{26,27},{30,31}} | collective-permute-start | bytes 786440 | tf_op jit(solution)/shard_map/ppermute | solution.py:675
  53.7 0.7 collective-permute-start.5
  54.4 0.7 collective-permute-start.4
  55.0 0.0 collective-permute-done.6.refs_3_
  55.1 0.6 collective-permute-start.9
  55.7 1.3 %pad_add_fusion.1.flags = s32[3]{0:T(128)S(1)} fusion(s32[1]{0:T(128)} %bitcast.23, s32[1]{0:T(128)} %bitcast.22, s32[1]{0:T(128)} %bitcast.21), kind=kLoop, calls=%fused_computation.22 | loop fusion | flops 6 | bytes 24 | tf_op jit(solution)/shard_map/stack | solution.py:702
  57.0 20.7 %shard_map.47 = (f32[2048,1024]{1,0:T(8,128)}, s32[32]{0:T(128)S(1)}, s32[19]{0:T(128)S(1)}, s32[128]{0:T(128)S(1)}) custom-call(s32[7]{0:T(128)S(1)} %stack.32.spot, s32[32,2,128]{2,1,0:T(2,128)S(1)} %slice_convert_fusion.tables, bf16[32,128,128]{2,1,0:T(8,128)(2,1)S(1)} %all-to-all-done.1.received.refs_2_, bf16[128,128,128]{2,1,0:T(8,128)(2,1)} %bitcast.39), custom_call_target="tpu_custom_call" | custom-call | flops 805306368 | bytes 16777216 | tf_op jit(solution)/shard_map/pallas_call | solution.py:515
  77.7 0.0 collective-permute-done.5.refs_2_
  77.7 0.0 collective-permute-done.4.refs_1_
  77.7 0.0 collective-permute-done.3.refs_0_
  77.7 25.8 %collective-permute-done.8.refs_5_ = bf16[70,128,128]{2,1,0:T(8,128)(2,1)} collective-permute-done((bf16[70,128,128]{2,1,0:T(8,128)(2,1)}, bf16[70,128,128]{2,1,0:T(8,128)(2,1)}, u32[]{:S(2)}, u32[]{:S(2)}) %collective-permute-start.8) | collective-permute-done | bytes 2293792 | tf_op jit(solution)/shard_map/ppermute | solution.py:657
  103.6 0.0 copy-done
  103.6 11.4 %shard_map.52 = (f32[2048,1024]{1,0:T(8,128)}, bf16[2048,1024]{1,0:T(8,128)(2,1)}, bf16[16,128,128]{2,1,0:T(8,128)(2,1)}, s32[16]{0:T(128)S(1)}, s32[16]{0:T(128)S(1)}) custom-call(s32[32]{0:T(128)S(1)} %get-tuple-element.55.order, s32[19]{0:T(128)S(1)} %get-tuple-element.56.first, s32[128]{0:T(128)S(1)} %get-tuple-element.57.target, ...), custom_call_target="tpu_custom_call" | custom-call | flops 536870912 | bytes 12582912 | tf_op jit(solution)/shard_map/pallas_call | solution.py:706
  115.0 0.1 collective-permute-start.10
  115.1 2.9 %collective-permute-done.9.refs_5_ = bf16[22,128,128]{2,1,0:T(8,128)(2,1)S(1)} collective-permute-done((bf16[22,128,128]{2,1,0:T(8,128)(2,1)}, bf16[22,128,128]{2,1,0:T(8,128)(2,1)S(1)}, u32[]{:S(2)}, u32[]{:S(2)}) %collective-permute-start.9) | collective-permute-done | bytes 720928 | tf_op jit(solution)/shard_map/ppermute | solution.py:657
  118.0 0.0 collective-permute-done.10.refs_6_
  118.0 0.0 copy-done.2
  118.0 0.0 copy-done.3
  118.0 0.0 copy-done.4
  118.0 3.6 %shard_map.53 = bf16[2048,1024]{1,0:T(8,128)(2,1)} custom-call(s32[32]{0:T(128)S(1)} %get-tuple-element.55.order, s32[19]{0:T(128)S(1)} %get-tuple-element.56.first, s32[128]{0:T(128)S(1)} %get-tuple-element.57.target, s32[3]{0:T(128)S(1)} %pad_add_fusion.1.flags, s32[16]{0:T(128)S(1)} %get-tuple-element.66.touched, ...), custom_call_target="tpu_custom_call", output_to_operand_aliasing={{}: (17, {})} | custom-call | flops 536870912 | bytes 12582912 | tf_op jit(solution)/shard_map/pallas_call | solution.py:706
  (22 shorter events, 0.2 us)
Async XLA Ops:
  2.2 15.8 %all-to-all-start = ((bf16[32,48,128]{2,1,0:T(8,128)(2,1)}), bf16[32,48,128]{2,1,0:T(8,128)(2,1)S(1)}, u32[]{:S(2)}, u32[]{:S(2)}) async-start(bf16[32,48,128]{2,1,0:T(8,128)(2,1)} %shard_map.46), calls=%async_computation | async-start | bytes 786432 | tf_op jit(solution)/shard_map/all_to_all | solution.py:622
  18.0 29.9 %all-to-all-start.1 = ((bf16[32,128,128]{2,1,0:T(8,128)(2,1)}), bf16[32,128,128]{2,1,0:T(8,128)(2,1)S(1)}, u32[]{:S(2)}, u32[]{:S(2)}) async-start(bf16[32,128,128]{2,1,0:T(8,128)(2,1)} %slice_bitcast_fusion), calls=%async_computation.1 | async-start | bytes 2097152 | tf_op jit(solution)/shard_map/all_to_all | solution.py:654
  33.7 3.4 %collective-permute-start.7 = (bf16[16,128,128]{2,1,0:T(8,128)(2,1)}, bf16[16,128,128]{2,1,0:T(8,128)(2,1)S(1)}, u32[]{:S(2)}, u32[]{:S(2)}) collective-permute-start(bf16[16,128,128]{2,1,0:T(8,128)(2,1)} %get-tuple-element.58.refs_1_), channel_id=1, source_target_pairs={{0,1},{1,0},{2,3},{3,2},{4,5},{5,4},{6,7},{7,6},{8,9},{9,8},{10,11... | collective-permute-start | bytes 1572872 | tf_op jit(solution)/shard_map/ppermute | solution.py:607
  37.2 13.9 %copy-start.1 = (bf16[16,128,128]{2,1,0:T(8,128)(2,1)S(1)}, bf16[16,128,128]{2,1,0:T(8,128)(2,1)}, u32[]{:S(2)}) copy-start(bf16[16,128,128]{2,1,0:T(8,128)(2,1)} %get-tuple-element.58.refs_1_) | copy-start | bytes 1572868
  47.9 55.7 %collective-permute-start.8 = (bf16[70,128,128]{2,1,0:T(8,128)(2,1)}, bf16[70,128,128]{2,1,0:T(8,128)(2,1)}, u32[]{:S(2)}, u32[]{:S(2)}) collective-permute-start(bf16[70,128,128]{2,1,0:T(8,128)(2,1)} %get-tuple-element.64), channel_id=1, source_target_pairs={{0,28},{4,0},{8,4},{12,8},{16,12},{20,16},{24,20},{28,24},{1,29},{... | collective-permute-start | bytes 6881288 | tf_op jit(solution)/shard_map/ppermute | solution.py:657
  48.4 29.3 %collective-permute-start.3 = (bf16[32,128,128]{2,1,0:T(8,128)(2,1)S(1)}, bf16[32,128,128]{2,1,0:T(8,128)(2,1)S(1)}, u32[]{:S(2)}, u32[]{:S(2)}) collective-permute-start(bf16[32,128,128]{2,1,0:T(8,128)(2,1)S(1)} %all-to-all-done.1.received.refs_2_), channel_id=1, source_target_pairs={{1,0},{2,1},{3,2},{5,4},{6,5},{7,6},{9,8},{10,9},{11,10},{13,12},{... | collective-permute-start | bytes 3145736 | tf_op jit(solution)/shard_map/ppermute | solution.py:673
  51.1 52.5 %copy-start = (bf16[32,32,128]{2,1,0:T(8,128)(2,1)S(1)}, bf16[32,32,128]{2,1,0:T(8,128)(2,1)}, u32[]{:S(2)}) copy-start(bf16[32,32,128]{2,1,0:T(8,128)(2,1)} %shard_map.49.refs_4_) | copy-start | bytes 786436
  51.1 4.0 %collective-permute-start.6 = (bf16[32,32,128]{2,1,0:T(8,128)(2,1)}, bf16[32,32,128]{2,1,0:T(8,128)(2,1)S(1)}, u32[]{:S(2)}, u32[]{:S(2)}) collective-permute-start(bf16[32,32,128]{2,1,0:T(8,128)(2,1)} %shard_map.49.refs_4_), channel_id=1, source_target_pairs={{2,3},{6,7},{10,11},{14,15},{18,19},{22,23},{26,27},{30,31}} | collective-permute-start | bytes 786440 | tf_op jit(solution)/shard_map/ppermute | solution.py:675
  53.7 24.0 %collective-permute-start.5 = (bf16[32,32,128]{2,1,0:T(8,128)(2,1)}, bf16[32,32,128]{2,1,0:T(8,128)(2,1)S(1)}, u32[]{:S(2)}, u32[]{:S(2)}) collective-permute-start(bf16[32,32,128]{2,1,0:T(8,128)(2,1)} %shard_map.49.refs_4_), channel_id=1, source_target_pairs={{1,3},{5,7},{9,11},{13,15},{17,19},{21,23},{25,27},{29,31}} | collective-permute-start | bytes 786440 | tf_op jit(solution)/shard_map/ppermute | solution.py:675
  54.4 23.4 %collective-permute-start.4 = (bf16[32,32,128]{2,1,0:T(8,128)(2,1)}, bf16[32,32,128]{2,1,0:T(8,128)(2,1)S(1)}, u32[]{:S(2)}, u32[]{:S(2)}) collective-permute-start(bf16[32,32,128]{2,1,0:T(8,128)(2,1)} %shard_map.49.refs_4_), channel_id=1, source_target_pairs={{0,3},{4,7},{8,11},{12,15},{16,19},{20,23},{24,27},{28,31}} | collective-permute-start | bytes 786440 | tf_op jit(solution)/shard_map/ppermute | solution.py:675
  55.1 63.0 %collective-permute-start.9 = (bf16[22,128,128]{2,1,0:T(8,128)(2,1)}, bf16[22,128,128]{2,1,0:T(8,128)(2,1)S(1)}, u32[]{:S(2)}, u32[]{:S(2)}) collective-permute-start(bf16[22,128,128]{2,1,0:T(8,128)(2,1)} %get-tuple-element.68), channel_id=1, source_target_pairs={{0,28},{4,0},{8,4},{12,8},{16,12},{20,16},{24,20},{28,24},{1,29},{... | collective-permute-start | bytes 2162696 | tf_op jit(solution)/shard_map/ppermute | solution.py:657
  103.6 14.5 %copy-start.2 = (bf16[20,128,128]{2,1,0:T(8,128)(2,1)S(1)}, bf16[20,128,128]{2,1,0:T(8,128)(2,1)}, u32[]{:S(2)}) copy-start(bf16[20,128,128]{2,1,0:T(8,128)(2,1)} %get-tuple-element.82.refs_9_) | copy-start | bytes 1966084
  103.6 14.5 %copy-start.3 = (bf16[8,128,128]{2,1,0:T(8,128)(2,1)S(1)}, bf16[8,128,128]{2,1,0:T(8,128)(2,1)}, u32[]{:S(2)}) copy-start(bf16[8,128,128]{2,1,0:T(8,128)(2,1)} %get-tuple-element.81.refs_8_) | copy-start | bytes 786436
  103.6 14.5 %copy-start.4 = (bf16[8,128,128]{2,1,0:T(8,128)(2,1)S(1)}, bf16[8,128,128]{2,1,0:T(8,128)(2,1)}, u32[]{:S(2)}) copy-start(bf16[8,128,128]{2,1,0:T(8,128)(2,1)} %get-tuple-element.80.refs_7_) | copy-start | bytes 786436
  115.0 3.0 %collective-permute-start.10 = (bf16[16,128,128]{2,1,0:T(8,128)(2,1)}, bf16[16,128,128]{2,1,0:T(8,128)(2,1)S(1)}, u32[]{:S(2)}, u32[]{:S(2)}) collective-permute-start(bf16[16,128,128]{2,1,0:T(8,128)(2,1)} %get-tuple-element.69), channel_id=1, source_target_pairs={{0,1},{1,0},{2,3},{3,2},{4,5},{5,4},{6,7},{7,6},{8,9},{9,8},{10,11... | collective-permute-start | bytes 1572872 | tf_op jit(solution)/shard_map/ppermute | solution.py:607
